TPU v7x, 32 devices: a whole 2x2x4 slice. The times are simulated.
32 devices in a mesh: section: 16 (over z, y, x), grp: 2 (over core).
Axes of the slice: x: 2, y: 2, z: 4, core: 2. Of those that a mesh axis runs over, the one named last changes fastest.
Arguments:
- planes: bfloat16 [4, 64, 64, 2048], P(None, 'section', None, 'grp'), may hold values from -6 to 6
- w_reduce: bfloat16 [3, 2048, 2048], P(None, None, 'grp'), may hold values from -0.125 to 0.125
- w_group: bfloat16 [3, 9, 32, 2048], P(None, None, None, 'grp'), may hold values from -0.375 to 0.375
- w_expand: bfloat16 [3, 2048, 2048], P(None, None, 'grp'), may hold values from -0.125 to 0.125
- gains: float32 [3, 3, 2048], P(None, None, 'grp'), may hold values from 0.25 to 1.75
- biases: float32 [3, 3, 2048], P(None, None, 'grp'), may hold values from -1.5 to 1.5
Outputs:
- feats: bfloat16 [4, 64, 64, 2048], P(None, 'section', None, 'grp')
All inputs are finite; a program needn't handle non-finite values.
Results may differ from a plain program's by a relative error of at most 0.014.
Values may be sent and summed in bfloat16 or wider, within the bound.
A program may use at most 192 MiB of HBM per device.

v0:
```python
import jax
import jax.numpy as jnp
from jax import lax
from jax.sharding import PartitionSpec as P


def extended(cells, sides, width):
    for axis, dim in sides:
        count = lax.axis_size(axis)
        ends = count - 1
        head = lax.slice_in_dim(cells, 0, width, axis=dim)
        tail = lax.slice_in_dim(cells, cells.shape[dim] - width, cells.shape[dim], axis=dim)
        cells = jnp.concatenate(
            [
                lax.ppermute(tail, axis, [(i, (i + 1) % count) for i in range(ends)]),
                cells,
                lax.ppermute(head, axis, [((i + 1) % count, i) for i in range(ends)]),
            ],
            axis=dim,
        )
    return cells


def group_matrix(kernel):
    tap_count, group_width, channels = kernel.shape
    tiled = jnp.tile(kernel, (1, channels // group_width, 1))
    row_group = lax.broadcasted_iota(jnp.int32, (channels, channels), 0) // group_width
    col_group = lax.broadcasted_iota(jnp.int32, (channels, channels), 1) // group_width
    masked = jnp.where((row_group == col_group)[None], tiled, jnp.zeros_like(tiled))
    return masked.reshape(tap_count * channels, channels)


def contract(weight, piece):
    return jnp.dot(piece, weight, preferred_element_type=jnp.float32)


def gather_reduce(flat, weight):
    return contract(weight, lax.all_gather(flat, "grp", axis=1, tiled=True))


def gather_expand(flat, weight):
    return contract(weight, lax.all_gather(flat, "grp", axis=1, tiled=True))


def run_block(planes, w_reduce, kernel, w_expand, gains, biases):
    tiles, rows, breadth, channels = planes.shape
    dense_group = group_matrix(kernel)
    first = gather_reduce(planes.reshape(-1, channels), w_reduce)
    hidden = jnp.maximum(gains[0] * first + biases[0], 0.0).astype(jnp.bfloat16)
    hidden = extended(hidden.reshape(planes.shape), (("section", 1),), 1)
    padded = jnp.pad(hidden, ((0, 0), (0, 0), (1, 1), (0, 0)))
    shifted = [
        padded[:, row_shift : row_shift + rows, col_shift : col_shift + breadth, :]
        for row_shift in range(3)
        for col_shift in range(3)
    ]
    taps = jnp.concatenate(shifted, axis=-1).reshape(tiles * rows * breadth, 9 * channels)
    spatial = jnp.dot(taps, dense_group, preferred_element_type=jnp.float32)
    middle = jnp.maximum(gains[1] * spatial + biases[1], 0.0).astype(jnp.bfloat16)
    second = gather_expand(middle, w_expand)
    stream = planes.reshape(-1, channels).astype(jnp.float32)
    result = jnp.maximum(gains[2] * second + biases[2] + stream, 0.0)
    return result.astype(jnp.bfloat16).reshape(planes.shape)


def local(planes, w_reduce, w_group, w_expand, gains, biases):
    current = planes
    for block in range(w_reduce.shape[0]):
        current = run_block(
            current, w_reduce[block], w_group[block], w_expand[block], gains[block], biases[block]
        )
    return current


def solution(mesh):
    placed = (
        P(None, "section", None, "grp"),
        P(None, None, "grp"),
        P(None, None, None, "grp"),
        P(None, None, "grp"),
        P(None, None, "grp"),
        P(None, None, "grp"),
    )
    return jax.shard_map(
        local,
        mesh=mesh,
        in_specs=placed,
        out_specs=P(None, "section", None, "grp"),
        check_vma=False,
    )
```

profile of v0, /device:TPU:13, one launch (start us, length us, event | category | flops | bytes accessed | tf_op | source)
XLA Modules:
  0.0 375.7 jit_solution(8298806482815675656)
XLA Ops:
  11.9 12.5 %all-gather.7.cloned.1.call-done = bf16[1024,2048]{1,0:T(8,128)(2,1)} async-done(((bf16[1024,1024]{1,0:T(8,128)(2,1)}), bf16[1024,2048]{1,0:T(8,128)(2,1)}) %all-gather.7.cloned.1.call-update) | async-done | bytes 4194320 | tf_op jit(solution)/shard_map/all_gather | solution.py:38
  24.4 8.0 %maximum_convert_fusion.8 = bf16[1024,1024]{1,0:T(8,128)(2,1)S(1)} fusion(f32[1024]{0:T(1024)S(1)} %bitcast.163, f32[1024]{0:T(1024)S(1)} %bitcast.162, bf16[1024,2048]{1,0:T(8,128)(2,1)} %all-gather.7.cloned.1.call-done, bf16[3,2048,1024]{2,1,0:T(8,128)(2,1)} %param.7), kind=kOutput, calls=%fused_computation.32 | convolution fusion | flops 4299161600 | bytes 10493952 | tf_op jit(solution)/shard_map/dot_general | solution.py:34
  33.3 3.1 collective-permute-start
  36.4 3.3 collective-permute-start.1
  40.8 18.4 %bitcast_select_fusion = (bf16[9216,1024]{1,0:T(8,128)(2,1)}, bf16[9216,1024]{1,0:T(8,128)(2,1)}, bf16[9216,1024]{1,0:T(8,128)(2,1)}) fusion(pred[1024,1024]{1,0:T(8,128)(4,1)S(1)} %select_compare_fusion, bf16[9,32,1024]{2,1,0:T(8,128)(2,1)S(1)} %get-tuple-element.35, bf16[9,32,1024]{2,1,0:T(8,128)(2,1)S(1)} %get-tuple-element.37, ...), kind=kLoop, calls=%fused_computation | loop fusion | flops 28311552 | bytes 59441152 | tf_op jit(solution)/shard_map/jit(_where)/select_n | solution.py:29
  59.1 2.2 collective-permute-done.1
  62.7 4.0 %fusion.46 = (bf16[4,4,64,1024]{3,2,1,0:T(8,128)(2,1)S(1)}, bf16[4,4,64,1024]{3,2,1,0:T(8,128)(2,1)S(1)}, bf16[4,4,64,1024]{3,2,1,0:T(8,128)(2,1)S(1)}, bf16[4,4...) fusion(bf16[4,6,66,1024]{3,2,1,0:T(8,128)(2,1)S(1)} %fusion.28), kind=kLoop, calls=%fused_computation.91 | loop fusion | bytes 25165824 | tf_op jit(solution)/shard_map/slice | solution.py:53
  81.1 24.5 %maximum_convert_fusion.7 = bf16[1024,1024]{1,0:T(8,128)(2,1)} fusion(bf16[1024,9216]{1,0:T(8,128)(2,1)} %constant_dynamic-update-slice_fusion, bf16[9216,1024]{1,0:T(8,128)(2,1)S(1)} %bitcast.119, f32[1024]{0:T(1024)S(1)} %bitcast.161, f32[1024]{0:T(1024)S(1)} %bitcast.160), kind=kOutput, calls=%fused_computation.30 | convolution fusion | flops 19331547136 | bytes 39854080 | tf_op jit(solution)/shard_map/dot_general | solution.py:58
  106.0 14.1 %all-gather.9.cloned.1.call-done = bf16[1024,2048]{1,0:T(8,128)(2,1)} async-done(((bf16[1024,1024]{1,0:T(8,128)(2,1)}), bf16[1024,2048]{1,0:T(8,128)(2,1)}) %all-gather.9.cloned.1.call-update) | async-done | bytes 4194320 | tf_op jit(solution)/shard_map/all_gather | solution.py:42
  120.0 9.5 %maximum_convert_fusion.6 = bf16[1024,1024]{1,0:T(8,128)(2,1)} fusion(bf16[1024,1024]{1,0:T(8,128)(2,1)S(1)} %bitcast.145, f32[1024]{0:T(1024)S(1)} %bitcast.159, f32[1024]{0:T(1024)S(1)} %bitcast.158, bf16[1024,2048]{1,0:T(8,128)(2,1)} %all-gather.9.cloned.1.call-done, bf16[3,2048,1024]{2,1,0:T(8,128)(2,1)} %param.9), kind=kOutput, calls=%fused_computation.28 | convolution fusion | flops 4301258752 | bytes 12591104 | tf_op jit(solution)/shard_map/dot_general | solution.py:34
  129.6 14.9 %all-gather.11.cloned.1.call-done = bf16[1024,2048]{1,0:T(8,128)(2,1)} async-done(((bf16[1024,1024]{1,0:T(8,128)(2,1)}), bf16[1024,2048]{1,0:T(8,128)(2,1)}) %all-gather.11.cloned.1.call-update) | async-done | bytes 4194320 | tf_op jit(solution)/shard_map/all_gather | solution.py:38
  144.6 8.0 %maximum_convert_fusion.5 = bf16[1024,1024]{1,0:T(8,128)(2,1)S(1)} fusion(f32[1024]{0:T(1024)S(1)} %bitcast.157, f32[1024]{0:T(1024)S(1)} %bitcast.156, bf16[1024,2048]{1,0:T(8,128)(2,1)} %all-gather.11.cloned.1.call-done, bf16[3,2048,1024]{2,1,0:T(8,128)(2,1)} %param.7), kind=kOutput, calls=%fused_computation.26 | convolution fusion | flops 4299161600 | bytes 10493952 | tf_op jit(solution)/shard_map/dot_general | solution.py:34
  152.6 3.1 collective-permute-start.2
  155.7 3.5 collective-permute-start.3
  159.3 9.4 %collective-permute-done.2 = bf16[4,1,64,1024]{3,2,1,0:T(8,128)(2,1)S(1)} collective-permute-done((bf16[4,1,64,1024]{3,2,1,0:T(8,128)(2,1)S(1)}, bf16[4,1,64,1024]{3,2,1,0:T(8,128)(2,1)S(1)}, u32[]{:S(2)}, u32[]{:S(2)}) %collective-permute-start.2) | collective-permute-done | bytes 524320 | tf_op jit(solution)/shard_map/ppermute | solution.py:15
  168.7 11.8 %collective-permute-done.3 = bf16[4,1,64,1024]{3,2,1,0:T(8,128)(2,1)S(1)} collective-permute-done((bf16[4,1,64,1024]{3,2,1,0:T(8,128)(2,1)S(1)}, bf16[4,1,64,1024]{3,2,1,0:T(8,128)(2,1)S(1)}, u32[]{:S(2)}, u32[]{:S(2)}) %collective-permute-start.3) | collective-permute-done | bytes 524320 | tf_op jit(solution)/shard_map/ppermute | solution.py:17
  181.8 4.1 %fusion.45 = (bf16[4,4,64,1024]{3,2,1,0:T(8,128)(2,1)S(1)}, bf16[4,4,64,1024]{3,2,1,0:T(8,128)(2,1)S(1)}, bf16[4,4,64,1024]{3,2,1,0:T(8,128)(2,1)S(1)}, bf16[4,4...) fusion(bf16[4,6,66,1024]{3,2,1,0:T(8,128)(2,1)S(1)} %fusion.26), kind=kLoop, calls=%fused_computation.90 | loop fusion | bytes 25165824 | tf_op jit(solution)/shard_map/slice | solution.py:53
  197.3 1.6 constant_dynamic-update-slice_fusion.10
  200.7 24.5 %maximum_convert_fusion.4 = bf16[1024,1024]{1,0:T(8,128)(2,1)} fusion(bf16[1024,9216]{1,0:T(8,128)(2,1)} %constant_dynamic-update-slice_fusion.9, bf16[9216,1024]{1,0:T(8,128)(2,1)S(1)} %bitcast.117, f32[1024]{0:T(1024)S(1)} %bitcast.155, f32[1024]{0:T(1024)S(1)} %bitcast.154), kind=kOutput, calls=%fused_computation.25 | convolution fusion | flops 19331547136 | bytes 39854080 | tf_op jit(solution)/shard_map/dot_general | solution.py:58
  225.3 14.3 %all-gather.13.cloned.1.call-done = bf16[1024,2048]{1,0:T(8,128)(2,1)} async-done(((bf16[1024,1024]{1,0:T(8,128)(2,1)}), bf16[1024,2048]{1,0:T(8,128)(2,1)}) %all-gather.13.cloned.1.call-update) | async-done | bytes 4194320 | tf_op jit(solution)/shard_map/all_gather | solution.py:42
  239.6 9.5 %maximum_convert_fusion.3 = bf16[1024,1024]{1,0:T(8,128)(2,1)} fusion(bf16[1024,1024]{1,0:T(8,128)(2,1)S(1)} %copy-done.2, f32[1024]{0:T(1024)S(1)} %bitcast.153, f32[1024]{0:T(1024)S(1)} %bitcast.152, bf16[1024,2048]{1,0:T(8,128)(2,1)} %all-gather.13.cloned.1.call-done, bf16[3,2048,1024]{2,1,0:T(8,128)(2,1)} %param.9), kind=kOutput, calls=%fused_computation.23 | convolution fusion | flops 4301258752 | bytes 12591104 | tf_op jit(solution)/shard_map/dot_general | solution.py:34
  249.4 14.8 %all-gather.15.cloned.1.call-done = bf16[1024,2048]{1,0:T(8,128)(2,1)} async-done(((bf16[1024,1024]{1,0:T(8,128)(2,1)}), bf16[1024,2048]{1,0:T(8,128)(2,1)}) %all-gather.15.cloned.1.call-update) | async-done | bytes 4194320 | tf_op jit(solution)/shard_map/all_gather | solution.py:38
  264.2 8.0 %maximum_convert_fusion.2 = bf16[1024,1024]{1,0:T(8,128)(2,1)S(1)} fusion(f32[1024]{0:T(1024)S(1)} %bitcast.151, f32[1024]{0:T(1024)S(1)} %bitcast.150, bf16[1024,2048]{1,0:T(8,128)(2,1)} %all-gather.15.cloned.1.call-done, bf16[3,2048,1024]{2,1,0:T(8,128)(2,1)} %param.7), kind=kOutput, calls=%fused_computation.21 | convolution fusion | flops 4299161600 | bytes 10493952 | tf_op jit(solution)/shard_map/dot_general | solution.py:34
  272.2 3.1 collective-permute-start.4
  275.3 3.1 collective-permute-start.5
  278.4 9.9 %collective-permute-done.4 = bf16[4,1,64,1024]{3,2,1,0:T(8,128)(2,1)S(1)} collective-permute-done((bf16[4,1,64,1024]{3,2,1,0:T(8,128)(2,1)S(1)}, bf16[4,1,64,1024]{3,2,1,0:T(8,128)(2,1)S(1)}, u32[]{:S(2)}, u32[]{:S(2)}) %collective-permute-start.4) | collective-permute-done | bytes 524320 | tf_op jit(solution)/shard_map/ppermute | solution.py:15
  288.3 11.8 %collective-permute-done.5 = bf16[4,1,64,1024]{3,2,1,0:T(8,128)(2,1)S(1)} collective-permute-done((bf16[4,1,64,1024]{3,2,1,0:T(8,128)(2,1)S(1)}, bf16[4,1,64,1024]{3,2,1,0:T(8,128)(2,1)S(1)}, u32[]{:S(2)}, u32[]{:S(2)}) %collective-permute-start.5) | collective-permute-done | bytes 524320 | tf_op jit(solution)/shard_map/ppermute | solution.py:17
  301.4 4.1 %fusion.44 = (bf16[4,4,64,1024]{3,2,1,0:T(8,128)(2,1)S(1)}, bf16[4,4,64,1024]{3,2,1,0:T(8,128)(2,1)S(1)}, bf16[4,4,64,1024]{3,2,1,0:T(8,128)(2,1)S(1)}, bf16[4,4...) fusion(bf16[4,6,66,1024]{3,2,1,0:T(8,128)(2,1)S(1)} %select_maximum_fusion), kind=kLoop, calls=%fused_computation.89 | loop fusion | bytes 25165824 | tf_op jit(solution)/shard_map/slice | solution.py:53
  309.1 1.6 constant_dynamic-update-slice_fusion.24
  320.3 24.5 %maximum_convert_fusion.1 = bf16[1024,1024]{1,0:T(8,128)(2,1)} fusion(bf16[1024,9216]{1,0:T(8,128)(2,1)} %constant_dynamic-update-slice_fusion.18, bf16[9216,1024]{1,0:T(8,128)(2,1)S(1)} %bitcast.115, f32[1024]{0:T(1024)S(1)} %bitcast.149, f32[1024]{0:T(1024)S(1)} %bitcast.148), kind=kOutput, calls=%fused_computation.20 | convolution fusion | flops 19331547136 | bytes 39854080 | tf_op jit(solution)/shard_map/dot_general | solution.py:58
  344.8 14.4 %all-gather.17.cloned.1.call-done = bf16[1024,2048]{1,0:T(8,128)(2,1)} async-done(((bf16[1024,1024]{1,0:T(8,128)(2,1)}), bf16[1024,2048]{1,0:T(8,128)(2,1)}) %all-gather.17.cloned.1.call-update) | async-done | bytes 4194320 | tf_op jit(solution)/shard_map/all_gather | solution.py:42
  359.2 9.5 %maximum_convert_fusion = bf16[1024,1024]{1,0:T(8,128)(2,1)} fusion(bf16[1024,1024]{1,0:T(8,128)(2,1)S(1)} %copy-done.1, f32[1024]{0:T(1024)S(1)} %bitcast.147, f32[1024]{0:T(1024)S(1)} %bitcast.146, bf16[1024,2048]{1,0:T(8,128)(2,1)} %all-gather.17.cloned.1.call-done, bf16[3,2048,1024]{2,1,0:T(8,128)(2,1)} %param.9), kind=kOutput, calls=%fused_computation.18 | convolution fusion | flops 4301258752 | bytes 12591104 | tf_op jit(solution)/shard_map/dot_general | solution.py:34
  (108 shorter events, 52.8 us)
Async XLA Ops:
  6.5 17.9 %all-gather.7.cloned.1.call-start = ((), (), s32[]{:S(2)}) async-start(), calls=%async_computation | async-start | bytes 6291456 | tf_op jit(solution)/shard_map/all_gather | solution.py:38
  7.3 112.8 %all-gather.9.cloned.1.call-start = ((), (), s32[]{:S(2)}) async-start(), calls=%async_computation.1 | async-start | bytes 6291456 | tf_op jit(solution)/shard_map/all_gather | solution.py:42
  33.3 25.9 %collective-permute-start = (bf16[4,1,64,1024]{3,2,1,0:T(8,128)(2,1)}, bf16[4,1,64,1024]{3,2,1,0:T(8,128)(2,1)S(1)}, u32[]{:S(2)}, u32[]{:S(2)}) collective-permute-start(bf16[4,1,64,1024]{3,2,1,0:T(8,128)(2,1)} %get-tuple-element.33), channel_id=1, source_target_pairs={{0,2},{2,4},{4,6},{6,8},{8,10},{10,12},{12,14},{14,16},{16,18},{18... | collective-permute-start | bytes 1572872 | tf_op jit(solution)/shard_map/ppermute | solution.py:15
  36.4 25.0 %collective-permute-start.1 = (bf16[4,1,64,1024]{3,2,1,0:T(8,128)(2,1)S(1)}, bf16[4,1,64,1024]{3,2,1,0:T(8,128)(2,1)S(1)}, u32[]{:S(2)}, u32[]{:S(2)}) collective-permute-start(bf16[4,1,64,1024]{3,2,1,0:T(8,128)(2,1)S(1)} %get-tuple-element.34), channel_id=1, source_target_pairs={{2,0},{4,2},{6,4},{8,6},{10,8},{12,10},{14,12},{16,14},{18,16},{20... | collective-permute-start | bytes 1572872 | tf_op jit(solution)/shard_map/ppermute | solution.py:17
  68.2 12.9 %slice-start.10 = ((s8[18874368]{0:T(1024)(128)(4,1)}), s8[4194304]{0:T(1024)(128)(4,1)S(1)}, s32[]{:S(2)}) async-start(s8[18874368]{0:T(1024)(128)(4,1)} %bitcast.118), calls=%async_computation.16 | async-start | bytes 8388608
  68.6 12.5 %slice-start.11 = ((s8[18874368]{0:T(1024)(128)(4,1)}), s8[4194304]{0:T(1024)(128)(4,1)S(1)}, s32[]{:S(2)}) async-start(s8[18874368]{0:T(1024)(128)(4,1)} %bitcast.118), calls=%async_computation.17 | async-start | bytes 8388608
  71.7 9.4 %slice-start.12 = ((s8[18874368]{0:T(1024)(128)(4,1)}), s8[4194304]{0:T(1024)(128)(4,1)S(1)}, s32[]{:S(2)}) async-start(s8[18874368]{0:T(1024)(128)(4,1)} %bitcast.118), calls=%async_computation.18 | async-start | bytes 8388608
  74.8 6.3 %slice-start.13 = ((s8[18874368]{0:T(1024)(128)(4,1)}), s8[4194304]{0:T(1024)(128)(4,1)S(1)}, s32[]{:S(2)}) async-start(s8[18874368]{0:T(1024)(128)(4,1)} %bitcast.118), calls=%async_computation.19 | async-start | bytes 8388608
  81.1 38.9 %copy-start = (bf16[4,4,64,1024]{3,2,1,0:T(8,128)(2,1)S(1)}, bf16[4,4,64,1024]{3,2,1,0:T(8,128)(2,1)}, u32[]{:S(2)}) copy-start(bf16[4,4,64,1024]{3,2,1,0:T(8,128)(2,1)} %param.6) | copy-start | bytes 6291460
  105.7 38.9 %all-gather.11.cloned.1.call-start = ((), (), s32[]{:S(2)}) async-start(), calls=%async_computation.2 | async-start | bytes 6291456 | tf_op jit(solution)/shard_map/all_gather | solution.py:38
  129.6 110.0 %all-gather.13.cloned.1.call-start = ((), (), s32[]{:S(2)}) async-start(), calls=%async_computation.3 | async-start | bytes 6291456 | tf_op jit(solution)/shard_map/all_gather | solution.py:42
  152.6 16.1 %collective-permute-start.2 = (bf16[4,1,64,1024]{3,2,1,0:T(8,128)(2,1)S(1)}, bf16[4,1,64,1024]{3,2,1,0:T(8,128)(2,1)S(1)}, u32[]{:S(2)}, u32[]{:S(2)}) collective-permute-start(bf16[4,1,64,1024]{3,2,1,0:T(8,128)(2,1)S(1)} %get-tuple-element.29), channel_id=1, source_target_pairs={{0,2},{2,4},{4,6},{6,8},{8,10},{10,12},{12,14},{14,16},{16,18},{18... | collective-permute-start | bytes 1572872 | tf_op jit(solution)/shard_map/ppermute | solution.py:15
  155.7 24.8 %collective-permute-start.3 = (bf16[4,1,64,1024]{3,2,1,0:T(8,128)(2,1)S(1)}, bf16[4,1,64,1024]{3,2,1,0:T(8,128)(2,1)S(1)}, u32[]{:S(2)}, u32[]{:S(2)}) collective-permute-start(bf16[4,1,64,1024]{3,2,1,0:T(8,128)(2,1)S(1)} %get-tuple-element.30), channel_id=1, source_target_pairs={{2,0},{4,2},{6,4},{8,6},{10,8},{12,10},{14,12},{16,14},{18,16},{20... | collective-permute-start | bytes 1572872 | tf_op jit(solution)/shard_map/ppermute | solution.py:17
  187.5 12.9 %slice-start.5 = ((s8[18874368]{0:T(1024)(128)(4,1)}), s8[2097152]{0:T(1024)(128)(4,1)S(1)}, s32[]{:S(2)}) async-start(s8[18874368]{0:T(1024)(128)(4,1)} %bitcast.116), calls=%async_computation.11 | async-start | bytes 4194304
  187.9 12.6 %slice-start.6 = ((s8[18874368]{0:T(1024)(128)(4,1)}), s8[4194304]{0:T(1024)(128)(4,1)S(1)}, s32[]{:S(2)}) async-start(s8[18874368]{0:T(1024)(128)(4,1)} %bitcast.116), calls=%async_computation.12 | async-start | bytes 8388608
  191.0 9.4 %slice-start.7 = ((s8[18874368]{0:T(1024)(128)(4,1)}), s8[4194304]{0:T(1024)(128)(4,1)S(1)}, s32[]{:S(2)}) async-start(s8[18874368]{0:T(1024)(128)(4,1)} %bitcast.116), calls=%async_computation.13 | async-start | bytes 8388608
  200.7 38.9 %copy-start.2 = (bf16[1024,1024]{1,0:T(8,128)(2,1)S(1)}, bf16[1024,1024]{1,0:T(8,128)(2,1)}, u32[]{:S(2)}) copy-start(bf16[1024,1024]{1,0:T(8,128)(2,1)} %maximum_convert_fusion.6) | copy-start | bytes 6291460
  200.7 38.9 %copy-start.9 = (f32[1,1,1024]{2,1,0:T(1,128)S(1)}, f32[1,1,1024]{2,1,0:T(1,128)}, u32[]{:S(2)}) copy-start(f32[1,1,1024]{2,1,0:T(1,128)} %get-tuple-element.45) | copy-start | bytes 12292
  200.7 38.9 %copy-start.10 = (f32[1,1,1024]{2,1,0:T(1,128)S(1)}, f32[1,1,1024]{2,1,0:T(1,128)}, u32[]{:S(2)}) copy-start(f32[1,1,1024]{2,1,0:T(1,128)} %get-tuple-element.52) | copy-start | bytes 12292
  225.2 38.9 %all-gather.15.cloned.1.call-start = ((), (), s32[]{:S(2)}) async-start(), calls=%async_computation.4 | async-start | bytes 6291456 | tf_op jit(solution)/shard_map/all_gather | solution.py:38
  239.6 24.5 %copy-start.7 = (f32[1,1,1024]{2,1,0:T(1,128)S(1)}, f32[1,1,1024]{2,1,0:T(1,128)}, u32[]{:S(2)}) copy-start(f32[1,1,1024]{2,1,0:T(1,128)} %get-tuple-element.46) | copy-start | bytes 12292
  239.6 24.5 %copy-start.8 = (f32[1,1,1024]{2,1,0:T(1,128)S(1)}, f32[1,1,1024]{2,1,0:T(1,128)}, u32[]{:S(2)}) copy-start(f32[1,1,1024]{2,1,0:T(1,128)} %get-tuple-element.51) | copy-start | bytes 12292
  249.2 110.1 %all-gather.17.cloned.1.call-start = ((), (), s32[]{:S(2)}) async-start(), calls=%async_computation.5 | async-start | bytes 6291456 | tf_op jit(solution)/shard_map/all_gather | solution.py:42
  272.2 16.1 %collective-permute-start.4 = (bf16[4,1,64,1024]{3,2,1,0:T(8,128)(2,1)S(1)}, bf16[4,1,64,1024]{3,2,1,0:T(8,128)(2,1)S(1)}, u32[]{:S(2)}, u32[]{:S(2)}) collective-permute-start(bf16[4,1,64,1024]{3,2,1,0:T(8,128)(2,1)S(1)} %get-tuple-element.25), channel_id=1, source_target_pairs={{0,2},{2,4},{4,6},{6,8},{8,10},{10,12},{12,14},{14,16},{16,18},{18... | collective-permute-start | bytes 1572872 | tf_op jit(solution)/shard_map/ppermute | solution.py:15
  275.3 24.8 %collective-permute-start.5 = (bf16[4,1,64,1024]{3,2,1,0:T(8,128)(2,1)S(1)}, bf16[4,1,64,1024]{3,2,1,0:T(8,128)(2,1)S(1)}, u32[]{:S(2)}, u32[]{:S(2)}) collective-permute-start(bf16[4,1,64,1024]{3,2,1,0:T(8,128)(2,1)S(1)} %get-tuple-element.26), channel_id=1, source_target_pairs={{2,0},{4,2},{6,4},{8,6},{10,8},{12,10},{14,12},{16,14},{18,16},{20... | collective-permute-start | bytes 1572872 | tf_op jit(solution)/shard_map/ppermute | solution.py:17
  307.1 13.0 %slice-start = ((s8[18874368]{0:T(1024)(128)(4,1)}), s8[2097152]{0:T(1024)(128)(4,1)S(1)}, s32[]{:S(2)}) async-start(s8[18874368]{0:T(1024)(128)(4,1)} %bitcast.114), calls=%async_computation.6 | async-start | bytes 4194304
  307.5 12.6 %slice-start.1 = ((s8[18874368]{0:T(1024)(128)(4,1)}), s8[4194304]{0:T(1024)(128)(4,1)S(1)}, s32[]{:S(2)}) async-start(s8[18874368]{0:T(1024)(128)(4,1)} %bitcast.114), calls=%async_computation.7 | async-start | bytes 8388608
  310.7 9.4 %slice-start.2 = ((s8[18874368]{0:T(1024)(128)(4,1)}), s8[4194304]{0:T(1024)(128)(4,1)S(1)}, s32[]{:S(2)}) async-start(s8[18874368]{0:T(1024)(128)(4,1)} %bitcast.114), calls=%async_computation.8 | async-start | bytes 8388608
  313.7 6.3 %slice-start.3 = ((s8[18874368]{0:T(1024)(128)(4,1)}), s8[4194304]{0:T(1024)(128)(4,1)S(1)}, s32[]{:S(2)}) async-start(s8[18874368]{0:T(1024)(128)(4,1)} %bitcast.114), calls=%async_computation.9 | async-start | bytes 8388608
  320.3 38.9 %copy-start.1 = (bf16[1024,1024]{1,0:T(8,128)(2,1)S(1)}, bf16[1024,1024]{1,0:T(8,128)(2,1)}, u32[]{:S(2)}) copy-start(bf16[1024,1024]{1,0:T(8,128)(2,1)} %maximum_convert_fusion.3) | copy-start | bytes 6291460
  320.3 38.9 %copy-start.3 = (f32[1,1,1024]{2,1,0:T(1,128)S(1)}, f32[1,1,1024]{2,1,0:T(1,128)}, u32[]{:S(2)}) copy-start(f32[1,1,1024]{2,1,0:T(1,128)} %get-tuple-element.47) | copy-start | bytes 12292
  320.3 38.9 %copy-start.4 = (f32[1,1,1024]{2,1,0:T(1,128)S(1)}, f32[1,1,1024]{2,1,0:T(1,128)}, u32[]{:S(2)}) copy-start(f32[1,1,1024]{2,1,0:T(1,128)} %get-tuple-element.58) | copy-start | bytes 12292
  (6 other events, 23.1 us)
Sparse Core Ops, SparseCore 0:
  8.9 15.4 all-gather.6
  105.8 14.2 all-gather.8
  129.7 14.8 all-gather.10
  225.4 14.2 all-gather.12
  249.3 14.8 all-gather.14
  345.0 14.2 all-gather.16
where the time goes:
time: 381 us; the launch traced here: 376 us
  waiting for transfers between devices  131 us (34%)
  matrix products  126 us (33%)
  local copies, waits for them, and re-layouts  60.6 us (16%)
  other arithmetic  24.6 us (6%)
  starting transfers between devices  19.8 us (5%)
  between operations  14 us (4%)
    dot_general x3, matrix products, run_block(): spatial = jnp.dot(taps, dense_group, preferred_element_type=jnp.float32)  73.5 us
    dot_general x6, matrix products, contract(): return jnp.dot(piece, weight, preferred_element_type=jnp.float32)  52.3 us
    all_gather x3, waiting for transfers between devices, gather_expand(): return contract(weight, lax.all_gather(flat, 'grp', axis=1, tiled=True))  42.8 us
    all_gather x3, waiting for transfers between devices, gather_reduce(): return contract(weight, lax.all_gather(flat, 'grp', axis=1, tiled=True))  42.2 us
    unnamed x76, local copies, waits for them, and re-layouts  38.1 us
    ppermute x3, waiting for transfers between devices, extended(): lax.ppermute(head, axis, [((i + 1) % count, i) for i in range(ends)])  25.7 us
    ppermute x3, waiting for transfers between devices, extended(): lax.ppermute(tail, axis, [(i, (i + 1) % count) for i in range(ends)])  19.4 us
    select_n x1, other arithmetic, group_matrix(): jnp.where((row_group == col_group)[None], tiled, jnp.zeros_like(tiled))  18.4 us
  transfers between devices with their start and end apart: 12, of which 11 were waited for; matrix products, arithmetic and copies ran while one was open for 6% of the time, Pallas kernels for 0%

commit v1 on v0

--- a/solution.py
+++ b/solution.py
@@ -1,6 +1,10 @@
+import functools
+
 import jax
 import jax.numpy as jnp
 from jax import lax
+from jax.experimental import pallas as pl
+from jax.experimental.pallas import tpu as pltpu
 from jax.sharding import PartitionSpec as P
 
 
@@ -72,6 +76,352 @@
     return current
 
 
+BLOCK = 256
+MESH = pl.DeviceIdType.MESH
+
+
+def fused_kernel(
+    count, planes, w_reduce, w_group, w_expand, gains, biases, out,
+    own, peer, mid, mid_peer, hid, halo, w_one, w_two, dense, taps,
+    local_sem, weight_sem, swap_send, swap_recv, lift_send, lift_recv,
+    cur_send, cur_recv, mid_send, mid_recv, halo_send, halo_recv, out_send, out_recv,
+):
+    blocks, depth, channels = w_reduce.shape[0], w_reduce.shape[1], planes.shape[2]
+    part = planes.shape[1]
+    whole = 2 * part
+    breadth = halo.shape[3]
+    pieces = channels // BLOCK
+    units = own.shape[0]
+    width = w_group.shape[1] // 9
+    section, core = lax.axis_index("section"), lax.axis_index("grp")
+    side = lax.rem(section, 2)
+    twin = section + 1 - 2 * side
+    above, below = section >= 2, section < count - 2
+    other_core = {"grp": 1 - core}
+    own_rows = pl.ds(pl.multiple_of(core * channels, channels), channels)
+    peer_rows = pl.ds(pl.multiple_of((1 - core) * channels, channels), channels)
+    mine = pl.ds(pl.multiple_of(side * part, part), part)
+    theirs = pl.ds(pl.multiple_of((1 - side) * part, part), part)
+
+    def remote(src, dst, send, recv, to):
+        return pltpu.make_async_remote_copy(
+            src_ref=src, dst_ref=dst, send_sem=send, recv_sem=recv, device_id=to, device_id_type=MESH)
+
+    def swap(unit):
+        return remote(planes.at[units * (1 - side) + unit], own.at[unit, mine],
+                      swap_send.at[unit], swap_recv.at[unit], {"section": twin})
+
+    def lift_first(unit):
+        return remote(planes.at[units * side + unit], peer.at[unit, mine],
+                      lift_send.at[0, unit], lift_recv.at[0, unit], other_core)
+
+    def lift_second(unit):
+        return remote(own.at[unit, theirs], peer.at[unit, theirs],
+                      lift_send.at[1, unit], lift_recv.at[1, unit], other_core)
+
+    def columns(piece):
+        return pl.ds(pl.multiple_of(piece * BLOCK, BLOCK), BLOCK)
+
+    def cur_copy(block, unit, piece):
+        return remote(own.at[unit, :, columns(piece)], peer.at[unit, :, columns(piece)],
+                      cur_send.at[block, unit, piece], cur_recv.at[block, unit, piece], other_core)
+
+    def mid_copy(block, unit, piece):
+        return remote(mid.at[unit, :, columns(piece)], mid_peer.at[unit, :, columns(piece)],
+                      mid_send.at[block, unit, piece], mid_recv.at[block, unit, piece], other_core)
+
+    def hid_columns(piece, shift):
+        return pl.ds(pl.multiple_of(piece * 3 * BLOCK + shift * BLOCK, BLOCK), BLOCK)
+
+    def halo_copy(block, unit, piece, edge):
+        start = breadth if edge == 0 else whole
+        return remote(hid.at[unit, pl.ds(start, breadth), hid_columns(piece, 1)],
+                      halo.at[block, unit, 1 - edge, :, columns(piece)],
+                      halo_send.at[block, unit, 1 - edge, piece], halo_recv.at[block, unit, 1 - edge, piece],
+                      {"section": section - 2 if edge == 0 else section + 2})
+
+    def outward(unit):
+        return remote(own.at[unit, theirs], out.at[units * side + unit],
+                      out_send.at[unit], out_recv.at[unit], {"section": twin})
+
+    def fetch(matrix, block, slots, at):
+        return pltpu.make_async_copy(matrix.at[block], slots.at[block % 2], weight_sem.at[at, block])
+
+    def each(body):
+        lax.fori_loop(0, pieces, lambda piece, carry: (body(piece), carry)[1], 0)
+
+    def dot(left, right):
+        return jnp.dot(left, right, preferred_element_type=jnp.float32)
+
+    def spread(unit, start, size, piece, values):
+        place = lax.broadcasted_iota(jnp.int32, values.shape, 0) & (breadth - 1)
+        rows = pl.ds(start, size)
+        before = jnp.where(place == 0, 0.0, pltpu.roll(values, 1, 0))
+        after = jnp.where(place == breadth - 1, 0.0, pltpu.roll(values, size - 1, 0))
+        hid[unit, rows, hid_columns(piece, 0)] = before.astype(jnp.bfloat16)
+        hid[unit, rows, hid_columns(piece, 1)] = values.astype(jnp.bfloat16)
+        hid[unit, rows, hid_columns(piece, 2)] = after.astype(jnp.bfloat16)
+
+    def reduce_rows(block, unit, rows, size, start, top, bottom):
+        def body(piece):
+            cols = columns(piece)
+            total = dot(own[unit, rows, :], w_one[block % 2, own_rows, cols])
+            total += dot(peer[unit, rows, :], w_one[block % 2, peer_rows, cols])
+            values = jnp.maximum(gains[3 * block, cols] * total + biases[3 * block, cols], 0.0)
+            spread(unit, start, size, piece, values)
+
+            @pl.when(jnp.logical_and(top, above))
+            def _():
+                halo_copy(block, unit, piece, 0).start()
+
+            @pl.when(jnp.logical_and(bottom, below))
+            def _():
+                halo_copy(block, unit, piece, 1).start()
+
+        each(body)
+
+    def reduce_mine(unit):
+        lift_first(unit).wait_recv()
+        reduce_rows(0, unit, mine, part, pl.multiple_of(breadth + side * part, breadth), side == 0, side == 1)
+
+    def receive(unit):
+        swap(unit).wait_recv()
+        lift_second(unit).start()
+
+    def reduce_theirs(unit):
+        lift_second(unit).wait_recv()
+        reduce_rows(0, unit, theirs, part, pl.multiple_of(breadth + (1 - side) * part, breadth), side == 1, side == 0)
+
+    def settle_halo(block, unit):
+        def body(piece):
+            @pl.when(above)
+            def _():
+                halo_copy(block, unit, piece, 0).wait_send()
+
+            @pl.when(below)
+            def _():
+                halo_copy(block, unit, piece, 1).wait_send()
+
+        each(body)
+
+    def reduce_all(block, unit):
+        each(lambda piece: cur_copy(block, unit, piece).wait_recv())
+        settle_halo(block - 1, unit)
+        reduce_rows(block, unit, slice(None), whole, breadth, True, True)
+
+    def convolve(block, unit):
+        if block > 0:
+            each(lambda piece: mid_copy(block - 1, unit, piece).wait_send())
+
+        def body(piece):
+            cols = columns(piece)
+
+            @pl.when(above)
+            def _():
+                halo_copy(block, unit, piece, 1).wait_recv()
+                spread(unit, 0, breadth, piece, halo[block, unit, 0, :, cols].astype(jnp.float32))
+
+            @pl.when(below)
+            def _():
+                halo_copy(block, unit, piece, 0).wait_recv()
+                spread(unit, whole + breadth, breadth, piece, halo[block, unit, 1, :, cols].astype(jnp.float32))
+
+            band = pl.ds(pl.multiple_of(piece * 3 * BLOCK, BLOCK), 3 * BLOCK)
+            total = None
+            for shift in range(3):
+                term = dot(hid[unit, pl.ds(shift * breadth, whole), band],
+                           dense[block % 2, pl.ds(shift * 3 * BLOCK, 3 * BLOCK), cols])
+                total = term if total is None else total + term
+            values = jnp.maximum(gains[3 * block + 1, cols] * total + biases[3 * block + 1, cols], 0.0)
+            mid[unit, :, cols] = values.astype(jnp.bfloat16)
+            mid_copy(block, unit, piece).start()
+
+        each(body)
+
+    def expand(block, unit):
+        each(lambda piece: mid_copy(block, unit, piece).wait_recv())
+        if block == 0:
+            lift_second(unit).wait_send()
+        else:
+            each(lambda piece: cur_copy(block, unit, piece).wait_send())
+
+        def body(piece):
+            cols = columns(piece)
+            total = dot(mid[unit], w_two[block % 2, own_rows, cols])
+            total += dot(mid_peer[unit], w_two[block % 2, peer_rows, cols])
+            total = gains[3 * block + 2, cols] * total + biases[3 * block + 2, cols]
+            values = jnp.maximum(total + own[unit, :, cols].astype(jnp.float32), 0.0)
+            own[unit, :, cols] = values.astype(jnp.bfloat16)
+            if block < blocks - 1:
+                cur_copy(block + 1, unit, piece).start()
+
+        each(body)
+        if block == blocks - 1:
+            outward(unit).start()
+            home(unit).start()
+
+    def home(unit):
+        return pltpu.make_async_copy(own.at[unit, mine], out.at[units * side + unit], local_sem.at[unit])
+
+    def stage(unit):
+        return pltpu.make_async_copy(planes.at[units * side + unit], own.at[unit, mine], local_sem.at[unit])
+
+    def build(block):
+        row = lax.broadcasted_iota(jnp.int32, (BLOCK, BLOCK), 0)
+        col = lax.broadcasted_iota(jnp.int32, (BLOCK, BLOCK), 1)
+        same = (row // width) == (col // width)
+
+        def tap_body(tap, carry):
+            source = pl.ds(pl.multiple_of(tap * width, width), width)
+            target = pl.ds(pl.multiple_of(tap * BLOCK, BLOCK), BLOCK)
+            for piece in range(pieces):
+                cols = pl.ds(piece * BLOCK, BLOCK)
+                values = taps[block, source, cols].astype(jnp.float32)
+                tiled = jnp.concatenate([values] * (BLOCK // width), axis=0)
+                dense[block % 2, target, cols] = jnp.where(same, tiled, 0.0).astype(jnp.bfloat16)
+            return carry
+
+        lax.fori_loop(0, 9, tap_body, 0)
+
+    barrier = pltpu.get_barrier_semaphore()
+    pl.semaphore_signal(barrier, inc=1, device_id=other_core, device_id_type=MESH)
+    pl.semaphore_signal(barrier, inc=1, device_id={"section": twin}, device_id_type=MESH)
+
+    @pl.when(above)
+    def _():
+        pl.semaphore_signal(barrier, inc=1, device_id={"section": section - 2}, device_id_type=MESH)
+
+    @pl.when(below)
+    def _():
+        pl.semaphore_signal(barrier, inc=1, device_id={"section": section + 2}, device_id_type=MESH)
+
+    for unit in range(units):
+        stage(unit).start()
+    group_load = pltpu.make_async_copy(w_group, taps, local_sem.at[units])
+    fetch(w_reduce, 0, w_one, 0).start()
+    group_load.start()
+    fetch(w_expand, 0, w_two, 1).start()
+    fetch(w_reduce, 1, w_one, 0).start()
+    fetch(w_expand, 1, w_two, 1).start()
+
+    pl.semaphore_wait(barrier, 2 + above.astype(jnp.int32) + below.astype(jnp.int32))
+
+    for unit in range(units):
+        swap(unit).start()
+    for unit in range(units):
+        lift_first(unit).start()
+    edge_zeros = jnp.zeros((breadth, hid.shape[2]), hid.dtype)
+    for unit in range(units):
+        hid[unit, pl.ds(0, breadth), :] = edge_zeros
+        hid[unit, pl.ds(whole + breadth, breadth), :] = edge_zeros
+    for unit in range(units):
+        stage(unit).wait()
+    fetch(w_reduce, 0, w_one, 0).wait()
+    reduce_mine(0)
+    reduce_mine(1)
+    group_load.wait()
+    build(0)
+    build(1)
+    fetch(w_expand, 0, w_two, 1).wait()
+    fetch(w_reduce, 1, w_one, 0).wait()
+    fetch(w_expand, 1, w_two, 1).wait()
+
+    receive(0)
+    reduce_theirs(0)
+    convolve(0, 0)
+    expand(0, 0)
+    reduce_all(1, 0)
+    receive(1)
+    convolve(1, 0)
+    reduce_theirs(1)
+    fetch(w_reduce, 2, w_one, 0).start()
+    expand(1, 0)
+    convolve(0, 1)
+    build(2)
+    fetch(w_reduce, 2, w_one, 0).wait()
+    reduce_all(2, 0)
+    expand(0, 1)
+    fetch(w_expand, 2, w_two, 1).start()
+    reduce_all(1, 1)
+    convolve(2, 0)
+    convolve(1, 1)
+    fetch(w_expand, 2, w_two, 1).wait()
+    expand(2, 0)
+    expand(1, 1)
+    reduce_all(2, 1)
+    convolve(2, 1)
+    expand(2, 1)
+
+    for unit in range(units):
+        settle_halo(blocks - 1, unit)
+        each(lambda piece: mid_copy(blocks - 1, unit, piece).wait_send())
+        swap(unit).wait_send()
+        lift_first(unit).wait_send()
+        home(unit).wait()
+        outward(unit).wait_send()
+        outward(unit).wait_recv()
+
+
+def fused(mesh):
+    count = mesh.shape["section"]
+
+    def call(planes, w_reduce, w_group, w_expand, gains, biases):
+        tiles, rows, breadth, channels = planes.shape
+        blocks, depth, _ = w_reduce.shape
+        part, units, pieces = rows * breadth, tiles // 2, channels // BLOCK
+        whole, kind = 2 * part, planes.dtype
+        dma = pltpu.SemaphoreType.DMA
+        scratch = [
+            pltpu.VMEM((units, whole, channels), kind),
+            pltpu.VMEM((units, whole, channels), kind),
+            pltpu.VMEM((units, whole, channels), kind),
+            pltpu.VMEM((units, whole, channels), kind),
+            pltpu.VMEM((units, whole + 2 * breadth, 3 * channels), kind),
+            pltpu.VMEM((blocks, units, 2, breadth, channels), kind),
+            pltpu.VMEM((2, depth, channels), kind),
+            pltpu.VMEM((2, depth, channels), kind),
+            pltpu.VMEM((2, 9 * BLOCK, channels), kind),
+            pltpu.VMEM((blocks, 9 * w_group.shape[2], channels), kind),
+            dma((units + 1,)), dma((2, blocks)),
+            dma((units,)), dma((units,)),
+            dma((2, units)), dma((2, units)),
+            dma((blocks, units, pieces)), dma((blocks, units, pieces)),
+            dma((blocks, units, pieces)), dma((blocks, units, pieces)),
+            dma((blocks, units, 2, pieces)), dma((blocks, units, 2, pieces)),
+            dma((units,)), dma((units,)),
+        ]
+        anywhere, inside = pl.BlockSpec(memory_space=pl.ANY), pl.BlockSpec(memory_space=pltpu.VMEM)
+        pixels = tiles * part
+        flops = 2 * pixels * blocks * channels * (2 * depth + 9 * BLOCK)
+        result = pl.pallas_call(
+            functools.partial(fused_kernel, count),
+            out_shape=jax.ShapeDtypeStruct((tiles, part, channels), kind),
+            in_specs=[anywhere] * 4 + [inside] * 2,
+            out_specs=anywhere,
+            scratch_shapes=scratch,
+            compiler_params=pltpu.CompilerParams(
+                collective_id=0, has_side_effects=True, vmem_limit_bytes=60 * 1024 * 1024),
+            cost_estimate=pl.CostEstimate(flops=flops, bytes_accessed=4 * blocks * depth * channels, transcendentals=0),
+        )(
+            planes.reshape(tiles, part, channels), w_reduce,
+            w_group.reshape(blocks, 9 * w_group.shape[2], channels), w_expand,
+            gains.reshape(blocks * 3, channels), biases.reshape(blocks * 3, channels),
+        )
+        return result.reshape(planes.shape)
+
+    return call
+
+
+def suits(mesh, planes, w_reduce, w_group):
+    tiles, rows, breadth, channels = planes.shape
+    return (
+        mesh.shape["grp"] == 2 and mesh.shape["section"] % 2 == 0 and tiles == 4
+        and channels % BLOCK == 0 and w_reduce.shape[0] == 3
+        and breadth % 16 == 0 and breadth & (breadth - 1) == 0
+        and w_group.shape[2] % 16 == 0 and BLOCK % w_group.shape[2] == 0
+    )
+
+
 def solution(mesh):
     placed = (
         P(None, "section", None, "grp"),
@@ -81,8 +431,13 @@
         P(None, None, "grp"),
         P(None, None, "grp"),
     )
+
+    def chosen(planes, w_reduce, w_group, *rest):
+        body = fused(mesh) if suits(mesh, planes, w_reduce, w_group) else local
+        return body(planes, w_reduce, w_group, *rest)
+
     return jax.shard_map(
-        local,
+        chosen,
         mesh=mesh,
         in_specs=placed,
         out_specs=P(None, "section", None, "grp"),

time: 381 us -> 110 us (0.29)
  waiting for transfers between devices: 131 us -> 0 us
  matrix products: 126 us -> 0 us
  Pallas kernels: 0 us -> 102 us
  local copies, waits for them, and re-layouts: 60.6 us -> 6.02 us
  other arithmetic: 24.6 us -> 0 us
  starting transfers between devices: 19.8 us -> 0 us
  between operations: 14 us -> 0.01 us
    dot_general x9 -> x0, matrix products: 126 us -> none  [the longest x3 73.5 us: run_block(): spatial = jnp.dot(taps, dense_group, preferred_element_type=jnp.float32)]
    pallas_call x0 -> x1, Pallas kernels: none -> 102 us  [call(): pl.pallas_call(functools.partial(fused_kernel, count), out_shape=jax.Shap...]
    all_gather x6 -> x0, waiting for transfers between devices: 85 us -> none  [the longest x3 42.8 us: gather_expand(): return contract(weight, lax.all_gather(flat, 'grp', axis=1, tiled=True))]
    ppermute x6 -> x0, waiting for transfers between devices: 45.1 us -> none  [the longest x3 25.7 us: extended(): lax.ppermute(head, axis, [((i + 1) % count, i) for i in range(ends)])]
    unnamed x76 -> x1, local copies, waits for them, and re-layouts: 38.1 us -> 3.14 us
    ppermute x6 -> x0, starting transfers between devices: 19.2 us -> none  [the longest x3 9.93 us: extended(): lax.ppermute(head, axis, [((i + 1) % count, i) for i in range(ends)])]
    select_n x1 -> x0, other arithmetic: 18.4 us -> none  [group_matrix(): jnp.where((row_group == col_group)[None], tiled, jnp.zeros_like(tiled))]
    slice x8 -> x0, local copies, waits for them, and re-layouts: 16.2 us -> none  [the longest x3 12.2 us: run_block(): padded[:, row_shift:row_shift + rows, col_shift:col_shift + breadth, :]]
  transfers between devices with their start and end apart: 12 -> 0, of which waited for: 11 -> 0; matrix products, arithmetic and copies ran while one was open for 6% -> 0% of each run, Pallas kernels for 0% -> 0%
where the time goes in v1:
time: 110 us; the launch traced here: 108 us
  Pallas kernels  102 us (93%)
  local copies, waits for them, and re-layouts  6.02 us (5%)
    pallas_call x1, Pallas kernels, call(): pl.pallas_call(functools.partial(fused_kernel, count), out_shape=jax.Shap...  102 us
    unnamed x1, local copies, waits for them, and re-layouts  3.14 us

profile of v1, /device:TPU:13, one launch (start us, length us, event | category | flops | bytes accessed | tf_op | source)
XLA Modules:
  0.0 108.4 jit_solution(16530136260662483545)
XLA Ops:
  0.0 1.4 %reshape.17.gains = f32[9,1024]{1,0:T(8,128)} reshape(f32[3,3,1024]{2,1,0:T(4,128)} %param.10) | data formatting | bytes 73728 | tf_op jit(solution)/shard_map/reshape | solution.py:408
  1.4 1.4 %reshape.18.biases = f32[9,1024]{1,0:T(8,128)} reshape(f32[3,3,1024]{2,1,0:T(4,128)} %param.11) | data formatting | bytes 73728 | tf_op jit(solution)/shard_map/reshape | solution.py:408
  2.9 102.4 %shard_map.64 = bf16[4,256,1024]{2,1,0:T(8,128)(2,1)} custom-call(bf16[4,256,1024]{2,1,0:T(8,128)(2,1)} %bitcast.4, bf16[3,2048,1024]{2,1,0:T(8,128)(2,1)} %w_reduce.1, bf16[3,288,1024]{2,1,0:T(8,128)(2,1)} %bitcast.5, bf16[3,2048,1024]{2,1,0:T(8,128)(2,1)} %w_expand.1, f32[9,1024]{1,0:T(8,128)} %reshape.17.gains, f32[9,1024]{1,0:T(8,128)} %reshape.18.biases), custom_call_target="tpu_custom_call" | custom-call | flops 40265318400 | bytes 25165824 | tf_op jit(solution)/shard_map/pallas_call | solution.py:396
  105.3 3.1 %copy.8 = bf16[4,4,64,1024]{3,2,1,0:T(8,128)(2,1)} copy(bf16[4,4,64,1024]{3,2,1,0:T(8,128)(2,1)} %bitcast.3) | data formatting | bytes 4194304

commit v2 on v1

--- a/solution.py
+++ b/solution.py
@@ -82,7 +82,7 @@
 
 def fused_kernel(
     count, planes, w_reduce, w_group, w_expand, gains, biases, out,
-    own, peer, mid, mid_peer, hid, halo, w_one, w_two, dense, taps,
+    cur, mid, hid, halo, w_one, w_two, dense, taps,
     local_sem, weight_sem, swap_send, swap_recv, lift_send, lift_recv,
     cur_send, cur_recv, mid_send, mid_recv, halo_send, halo_recv, out_send, out_recv,
 ):
@@ -91,15 +91,14 @@
     whole = 2 * part
     breadth = halo.shape[3]
     pieces = channels // BLOCK
-    units = own.shape[0]
+    units = cur.shape[0]
     width = w_group.shape[1] // 9
     section, core = lax.axis_index("section"), lax.axis_index("grp")
     side = lax.rem(section, 2)
     twin = section + 1 - 2 * side
     above, below = section >= 2, section < count - 2
     other_core = {"grp": 1 - core}
-    own_rows = pl.ds(pl.multiple_of(core * channels, channels), channels)
-    peer_rows = pl.ds(pl.multiple_of((1 - core) * channels, channels), channels)
+    own = pl.ds(pl.multiple_of(core * channels, channels), channels)
     mine = pl.ds(pl.multiple_of(side * part, part), part)
     theirs = pl.ds(pl.multiple_of((1 - side) * part, part), part)
 
@@ -108,26 +107,29 @@
             src_ref=src, dst_ref=dst, send_sem=send, recv_sem=recv, device_id=to, device_id_type=MESH)
 
     def swap(unit):
-        return remote(planes.at[units * (1 - side) + unit], own.at[unit, mine],
+        return remote(planes.at[units * (1 - side) + unit], cur.at[unit, mine, own],
                       swap_send.at[unit], swap_recv.at[unit], {"section": twin})
 
     def lift_first(unit):
-        return remote(planes.at[units * side + unit], peer.at[unit, mine],
+        return remote(planes.at[units * side + unit], cur.at[unit, mine, own],
                       lift_send.at[0, unit], lift_recv.at[0, unit], other_core)
 
     def lift_second(unit):
-        return remote(own.at[unit, theirs], peer.at[unit, theirs],
+        return remote(cur.at[unit, theirs, own], cur.at[unit, theirs, own],
                       lift_send.at[1, unit], lift_recv.at[1, unit], other_core)
 
     def columns(piece):
         return pl.ds(pl.multiple_of(piece * BLOCK, BLOCK), BLOCK)
 
+    def own_columns(piece):
+        return pl.ds(pl.multiple_of(core * channels + piece * BLOCK, BLOCK), BLOCK)
+
     def cur_copy(block, unit, piece):
-        return remote(own.at[unit, :, columns(piece)], peer.at[unit, :, columns(piece)],
+        return remote(cur.at[unit, :, own_columns(piece)], cur.at[unit, :, own_columns(piece)],
                       cur_send.at[block, unit, piece], cur_recv.at[block, unit, piece], other_core)
 
     def mid_copy(block, unit, piece):
-        return remote(mid.at[unit, :, columns(piece)], mid_peer.at[unit, :, columns(piece)],
+        return remote(mid.at[unit, :, own_columns(piece)], mid.at[unit, :, own_columns(piece)],
                       mid_send.at[block, unit, piece], mid_recv.at[block, unit, piece], other_core)
 
     def hid_columns(piece, shift):
@@ -140,15 +142,25 @@
                       halo_send.at[block, unit, 1 - edge, piece], halo_recv.at[block, unit, 1 - edge, piece],
                       {"section": section - 2 if edge == 0 else section + 2})
 
-    def outward(unit):
-        return remote(own.at[unit, theirs], out.at[units * side + unit],
-                      out_send.at[unit], out_recv.at[unit], {"section": twin})
+    def outward(unit, piece):
+        return remote(cur.at[unit, theirs, own_columns(piece)], out.at[units * side + unit, :, columns(piece)],
+                      out_send.at[unit, piece], out_recv.at[unit, piece], {"section": twin})
 
     def fetch(matrix, block, slots, at):
         return pltpu.make_async_copy(matrix.at[block], slots.at[block % 2], weight_sem.at[at, block])
 
     def each(body):
         lax.fori_loop(0, pieces, lambda piece, carry: (body(piece), carry)[1], 0)
+
+    def pairs(work, after):
+        def body(at, carry):
+            for piece in (2 * at, 2 * at + 1):
+                work(piece)
+            for piece in (2 * at, 2 * at + 1):
+                after(piece)
+            return carry
+
+        lax.fori_loop(0, pieces // 2, body, 0)
 
     def dot(left, right):
         return jnp.dot(left, right, preferred_element_type=jnp.float32)
@@ -165,11 +177,11 @@
     def reduce_rows(block, unit, rows, size, start, top, bottom):
         def body(piece):
             cols = columns(piece)
-            total = dot(own[unit, rows, :], w_one[block % 2, own_rows, cols])
-            total += dot(peer[unit, rows, :], w_one[block % 2, peer_rows, cols])
-            values = jnp.maximum(gains[3 * block, cols] * total + biases[3 * block, cols], 0.0)
+            total = dot(cur[unit, rows, :], w_one[block % 2, :, cols])
+            values = jnp.maximum(gains[block, 0, cols] * total + biases[block, 0, cols], 0.0)
             spread(unit, start, size, piece, values)
 
+        def after(piece):
             @pl.when(jnp.logical_and(top, above))
             def _():
                 halo_copy(block, unit, piece, 0).start()
@@ -178,7 +190,7 @@
             def _():
                 halo_copy(block, unit, piece, 1).start()
 
-        each(body)
+        pairs(body, after)
 
     def reduce_mine(unit):
         lift_first(unit).wait_recv()
@@ -186,6 +198,8 @@
 
     def receive(unit):
         swap(unit).wait_recv()
+        if unit + 1 < units:
+            swap(unit + 1).start()
         lift_second(unit).start()
 
     def reduce_theirs(unit):
@@ -213,30 +227,32 @@
         if block > 0:
             each(lambda piece: mid_copy(block - 1, unit, piece).wait_send())
 
+        def edges(piece):
+            cols = columns(piece)
+
+            @pl.when(above)
+            def _():
+                halo_copy(block, unit, piece, 1).wait_recv()
+                spread(unit, 0, breadth, piece, halo[block, unit, 0, :, cols].astype(jnp.float32))
+
+            @pl.when(below)
+            def _():
+                halo_copy(block, unit, piece, 0).wait_recv()
+                spread(unit, whole + breadth, breadth, piece, halo[block, unit, 1, :, cols].astype(jnp.float32))
+
         def body(piece):
             cols = columns(piece)
-
-            @pl.when(above)
-            def _():
-                halo_copy(block, unit, piece, 1).wait_recv()
-                spread(unit, 0, breadth, piece, halo[block, unit, 0, :, cols].astype(jnp.float32))
-
-            @pl.when(below)
-            def _():
-                halo_copy(block, unit, piece, 0).wait_recv()
-                spread(unit, whole + breadth, breadth, piece, halo[block, unit, 1, :, cols].astype(jnp.float32))
-
             band = pl.ds(pl.multiple_of(piece * 3 * BLOCK, BLOCK), 3 * BLOCK)
             total = None
             for shift in range(3):
                 term = dot(hid[unit, pl.ds(shift * breadth, whole), band],
                            dense[block % 2, pl.ds(shift * 3 * BLOCK, 3 * BLOCK), cols])
                 total = term if total is None else total + term
-            values = jnp.maximum(gains[3 * block + 1, cols] * total + biases[3 * block + 1, cols], 0.0)
-            mid[unit, :, cols] = values.astype(jnp.bfloat16)
-            mid_copy(block, unit, piece).start()
-
-        each(body)
+            values = jnp.maximum(gains[block, 1, cols] * total + biases[block, 1, cols], 0.0)
+            mid[unit, :, own_columns(piece)] = values.astype(jnp.bfloat16)
+
+        each(edges)
+        pairs(body, lambda piece: mid_copy(block, unit, piece).start())
 
     def expand(block, unit):
         each(lambda piece: mid_copy(block, unit, piece).wait_recv())
@@ -247,24 +263,26 @@
 
         def body(piece):
             cols = columns(piece)
-            total = dot(mid[unit], w_two[block % 2, own_rows, cols])
-            total += dot(mid_peer[unit], w_two[block % 2, peer_rows, cols])
-            total = gains[3 * block + 2, cols] * total + biases[3 * block + 2, cols]
-            values = jnp.maximum(total + own[unit, :, cols].astype(jnp.float32), 0.0)
-            own[unit, :, cols] = values.astype(jnp.bfloat16)
+            total = dot(mid[unit], w_two[block % 2, :, cols])
+            total = gains[block, 2, cols] * total + biases[block, 2, cols]
+            values = jnp.maximum(total + cur[unit, :, own_columns(piece)].astype(jnp.float32), 0.0)
+            cur[unit, :, own_columns(piece)] = values.astype(jnp.bfloat16)
+
+        def after(piece):
             if block < blocks - 1:
                 cur_copy(block + 1, unit, piece).start()
-
-        each(body)
+            else:
+                outward(unit, piece).start()
+
+        pairs(body, after)
         if block == blocks - 1:
-            outward(unit).start()
             home(unit).start()
 
     def home(unit):
-        return pltpu.make_async_copy(own.at[unit, mine], out.at[units * side + unit], local_sem.at[unit])
+        return pltpu.make_async_copy(cur.at[unit, mine, own], out.at[units * side + unit], local_sem.at[unit])
 
     def stage(unit):
-        return pltpu.make_async_copy(planes.at[units * side + unit], own.at[unit, mine], local_sem.at[unit])
+        return pltpu.make_async_copy(planes.at[units * side + unit], cur.at[unit, mine, own], local_sem.at[unit])
 
     def build(block):
         row = lax.broadcasted_iota(jnp.int32, (BLOCK, BLOCK), 0)
@@ -306,8 +324,7 @@
 
     pl.semaphore_wait(barrier, 2 + above.astype(jnp.int32) + below.astype(jnp.int32))
 
-    for unit in range(units):
-        swap(unit).start()
+    swap(0).start()
     for unit in range(units):
         lift_first(unit).start()
     edge_zeros = jnp.zeros((breadth, hid.shape[2]), hid.dtype)
@@ -358,8 +375,8 @@
         swap(unit).wait_send()
         lift_first(unit).wait_send()
         home(unit).wait()
-        outward(unit).wait_send()
-        outward(unit).wait_recv()
+        each(lambda piece: outward(unit, piece).wait_send())
+        each(lambda piece: outward(unit, piece).wait_recv())
 
 
 def fused(mesh):
@@ -372,10 +389,8 @@
         whole, kind = 2 * part, planes.dtype
         dma = pltpu.SemaphoreType.DMA
         scratch = [
-            pltpu.VMEM((units, whole, channels), kind),
-            pltpu.VMEM((units, whole, channels), kind),
-            pltpu.VMEM((units, whole, channels), kind),
-            pltpu.VMEM((units, whole, channels), kind),
+            pltpu.VMEM((units, whole, depth), kind),
+            pltpu.VMEM((units, whole, depth), kind),
             pltpu.VMEM((units, whole + 2 * breadth, 3 * channels), kind),
             pltpu.VMEM((blocks, units, 2, breadth, channels), kind),
             pltpu.VMEM((2, depth, channels), kind),
@@ -388,7 +403,7 @@
             dma((blocks, units, pieces)), dma((blocks, units, pieces)),
             dma((blocks, units, pieces)), dma((blocks, units, pieces)),
             dma((blocks, units, 2, pieces)), dma((blocks, units, 2, pieces)),
-            dma((units,)), dma((units,)),
+            dma((units, pieces)), dma((units, pieces)),
         ]
         anywhere, inside = pl.BlockSpec(memory_space=pl.ANY), pl.BlockSpec(memory_space=pltpu.VMEM)
         pixels = tiles * part
@@ -405,7 +420,7 @@
         )(
             planes.reshape(tiles, part, channels), w_reduce,
             w_group.reshape(blocks, 9 * w_group.shape[2], channels), w_expand,
-            gains.reshape(blocks * 3, channels), biases.reshape(blocks * 3, channels),
+            gains, biases,
         )
         return result.reshape(planes.shape)
 
@@ -416,7 +431,7 @@
     tiles, rows, breadth, channels = planes.shape
     return (
         mesh.shape["grp"] == 2 and mesh.shape["section"] % 2 == 0 and tiles == 4
-        and channels % BLOCK == 0 and w_reduce.shape[0] == 3
+        and channels % (2 * BLOCK) == 0 and w_reduce.shape[0] == 3
         and breadth % 16 == 0 and breadth & (breadth - 1) == 0
         and w_group.shape[2] % 16 == 0 and BLOCK % w_group.shape[2] == 0
     )

time: 110 us -> 115 us (1.045); the launches traced: 108 us -> 115 us
  Pallas kernels: 102 us -> 112 us
  local copies, waits for them, and re-layouts: 6.02 us -> 3.14 us
    pallas_call x1, Pallas kernels: 102 us -> 112 us  [call(): pl.pallas_call(functools.partial(fused_kernel, count), out_shape=jax.Shap...]
    reshape x2 -> x0, local copies, waits for them, and re-layouts: 2.88 us -> none  [the longest x1 1.45 us: call(): gains.reshape(blocks * 3, channels)]
where the time goes in v2:
time: 115 us
  Pallas kernels  112 us (97%)
  local copies, waits for them, and re-layouts  3.14 us (3%)
    pallas_call x1, Pallas kernels, call(): pl.pallas_call(functools.partial(fused_kernel, count), out_shape=jax.Shap...  112 us
    unnamed x1, local copies, waits for them, and re-layouts  3.14 us

profile of v2, /device:TPU:13, one launch (start us, length us, event | category | flops | bytes accessed | tf_op | source)
XLA Modules:
  0.0 115.1 jit_solution(1707786763015182972)
XLA Ops:
  0.0 112.0 %shard_map.64 = bf16[4,256,1024]{2,1,0:T(8,128)(2,1)} custom-call(bf16[4,256,1024]{2,1,0:T(8,128)(2,1)} %bitcast.4, bf16[3,2048,1024]{2,1,0:T(8,128)(2,1)} %w_reduce.1, bf16[3,288,1024]{2,1,0:T(8,128)(2,1)} %bitcast.5, bf16[3,2048,1024]{2,1,0:T(8,128)(2,1)} %w_expand.1, f32[3,3,1024]{2,1,0:T(4,128)} %gains.1, f32[3,3,1024]{2,1,0:T(4,128)} %biases.1), custom_call_target="tpu_custom_call" | custom-call | flops 40265318400 | bytes 25165824 | tf_op jit(solution)/shard_map/pallas_call | solution.py:411
  112.0 3.1 %copy.8 = bf16[4,4,64,1024]{3,2,1,0:T(8,128)(2,1)} copy(bf16[4,4,64,1024]{3,2,1,0:T(8,128)(2,1)} %bitcast.3) | data formatting | bytes 4194304

commit v3 on v2

--- a/solution.py
+++ b/solution.py
@@ -106,17 +106,24 @@
         return pltpu.make_async_remote_copy(
             src_ref=src, dst_ref=dst, send_sem=send, recv_sem=recv, device_id=to, device_id_type=MESH)
 
-    def swap(unit):
-        return remote(planes.at[units * (1 - side) + unit], cur.at[unit, mine, own],
-                      swap_send.at[unit], swap_recv.at[unit], {"section": twin})
+    lines = part // breadth
+
+    def line_rows(half, line):
+        return pl.ds(pl.multiple_of(half * part + line * breadth, breadth), breadth)
+
+    def swap(unit, line):
+        return remote(planes.at[units * (1 - side) + unit, pl.ds(line * breadth, breadth)],
+                      cur.at[unit, line_rows(side, line), own],
+                      swap_send.at[unit, line], swap_recv.at[unit, line], {"section": twin})
 
     def lift_first(unit):
         return remote(planes.at[units * side + unit], cur.at[unit, mine, own],
-                      lift_send.at[0, unit], lift_recv.at[0, unit], other_core)
-
-    def lift_second(unit):
-        return remote(cur.at[unit, theirs, own], cur.at[unit, theirs, own],
-                      lift_send.at[1, unit], lift_recv.at[1, unit], other_core)
+                      lift_send.at[unit, lines], lift_recv.at[unit, lines], other_core)
+
+    def lift_second(unit, line):
+        there = line_rows(1 - side, line)
+        return remote(cur.at[unit, there, own], cur.at[unit, there, own],
+                      lift_send.at[unit, line], lift_recv.at[unit, line], other_core)
 
     def columns(piece):
         return pl.ds(pl.multiple_of(piece * BLOCK, BLOCK), BLOCK)
@@ -197,13 +204,13 @@
         reduce_rows(0, unit, mine, part, pl.multiple_of(breadth + side * part, breadth), side == 0, side == 1)
 
     def receive(unit):
-        swap(unit).wait_recv()
-        if unit + 1 < units:
-            swap(unit + 1).start()
-        lift_second(unit).start()
+        for line in range(lines):
+            swap(unit, line).wait_recv()
+            lift_second(unit, line).start()
 
     def reduce_theirs(unit):
-        lift_second(unit).wait_recv()
+        for line in range(lines):
+            lift_second(unit, line).wait_recv()
         reduce_rows(0, unit, theirs, part, pl.multiple_of(breadth + (1 - side) * part, breadth), side == 1, side == 0)
 
     def settle_halo(block, unit):
@@ -257,7 +264,8 @@
     def expand(block, unit):
         each(lambda piece: mid_copy(block, unit, piece).wait_recv())
         if block == 0:
-            lift_second(unit).wait_send()
+            for line in range(lines):
+                lift_second(unit, line).wait_send()
         else:
             each(lambda piece: cur_copy(block, unit, piece).wait_send())
 
@@ -324,7 +332,8 @@
 
     pl.semaphore_wait(barrier, 2 + above.astype(jnp.int32) + below.astype(jnp.int32))
 
-    swap(0).start()
+    for line in range(lines):
+        swap(0, line).start()
     for unit in range(units):
         lift_first(unit).start()
     edge_zeros = jnp.zeros((breadth, hid.shape[2]), hid.dtype)
@@ -334,10 +343,12 @@
     for unit in range(units):
         stage(unit).wait()
     fetch(w_reduce, 0, w_one, 0).wait()
-    reduce_mine(0)
-    reduce_mine(1)
     group_load.wait()
     build(0)
+    reduce_mine(0)
+    for line in range(lines):
+        swap(1, line).start()
+    reduce_mine(1)
     build(1)
     fetch(w_expand, 0, w_two, 1).wait()
     fetch(w_reduce, 1, w_one, 0).wait()
@@ -372,7 +383,8 @@
     for unit in range(units):
         settle_halo(blocks - 1, unit)
         each(lambda piece: mid_copy(blocks - 1, unit, piece).wait_send())
-        swap(unit).wait_send()
+        for line in range(lines):
+            swap(unit, line).wait_send()
         lift_first(unit).wait_send()
         home(unit).wait()
         each(lambda piece: outward(unit, piece).wait_send())
@@ -398,8 +410,8 @@
             pltpu.VMEM((2, 9 * BLOCK, channels), kind),
             pltpu.VMEM((blocks, 9 * w_group.shape[2], channels), kind),
             dma((units + 1,)), dma((2, blocks)),
-            dma((units,)), dma((units,)),
-            dma((2, units)), dma((2, units)),
+            dma((units, rows)), dma((units, rows)),
+            dma((units, rows + 1)), dma((units, rows + 1)),
             dma((blocks, units, pieces)), dma((blocks, units, pieces)),
             dma((blocks, units, pieces)), dma((blocks, units, pieces)),
             dma((blocks, units, 2, pieces)), dma((blocks, units, 2, pieces)),

time: 115 us -> 116 us (level)
  no operation moved by 1% of the time
where the time goes in v3:
time: 116 us
  Pallas kernels  113 us (97%)
  local copies, waits for them, and re-layouts  3.14 us (3%)
    pallas_call x1, Pallas kernels, call(): pl.pallas_call(functools.partial(fused_kernel, count), out_shape=jax.Shap...  113 us
    unnamed x1, local copies, waits for them, and re-layouts  3.14 us

profile of v3, /device:TPU:13, one launch (start us, length us, event | category | flops | bytes accessed | tf_op | source)
XLA Modules:
  0.0 116.0 jit_solution(2918979378994005483)
XLA Ops:
  0.0 112.8 %shard_map.64 = bf16[4,256,1024]{2,1,0:T(8,128)(2,1)} custom-call(bf16[4,256,1024]{2,1,0:T(8,128)(2,1)} %bitcast.4, bf16[3,2048,1024]{2,1,0:T(8,128)(2,1)} %w_reduce.1, bf16[3,288,1024]{2,1,0:T(8,128)(2,1)} %bitcast.5, bf16[3,2048,1024]{2,1,0:T(8,128)(2,1)} %w_expand.1, f32[3,3,1024]{2,1,0:T(4,128)} %gains.1, f32[3,3,1024]{2,1,0:T(4,128)} %biases.1), custom_call_target="tpu_custom_call" | custom-call | flops 40265318400 | bytes 25165824 | tf_op jit(solution)/shard_map/pallas_call | solution.py:423
  112.8 3.1 %copy.8 = bf16[4,4,64,1024]{3,2,1,0:T(8,128)(2,1)} copy(bf16[4,4,64,1024]{3,2,1,0:T(8,128)(2,1)} %bitcast.3) | data formatting | bytes 4194304

commit v4 on v3

--- a/solution.py
+++ b/solution.py
@@ -159,15 +159,13 @@
     def each(body):
         lax.fori_loop(0, pieces, lambda piece, carry: (body(piece), carry)[1], 0)
 
-    def pairs(work, after):
+    def steps(work, after):
         def body(at, carry):
-            for piece in (2 * at, 2 * at + 1):
-                work(piece)
-            for piece in (2 * at, 2 * at + 1):
-                after(piece)
+            work(at)
+            after(at)
             return carry
 
-        lax.fori_loop(0, pieces // 2, body, 0)
+        lax.fori_loop(0, pieces, body, 0)
 
     def dot(left, right):
         return jnp.dot(left, right, preferred_element_type=jnp.float32)
@@ -184,7 +182,8 @@
     def reduce_rows(block, unit, rows, size, start, top, bottom):
         def body(piece):
             cols = columns(piece)
-            total = dot(cur[unit, rows, :], w_one[block % 2, :, cols])
+            total = dot(cur[unit, rows, :channels], w_one[block % 2, :channels, cols])
+            total += dot(cur[unit, rows, channels:], w_one[block % 2, channels:, cols])
             values = jnp.maximum(gains[block, 0, cols] * total + biases[block, 0, cols], 0.0)
             spread(unit, start, size, piece, values)
 
@@ -197,7 +196,7 @@
             def _():
                 halo_copy(block, unit, piece, 1).start()
 
-        pairs(body, after)
+        steps(body, after)
 
     def reduce_mine(unit):
         lift_first(unit).wait_recv()
@@ -259,7 +258,7 @@
             mid[unit, :, own_columns(piece)] = values.astype(jnp.bfloat16)
 
         each(edges)
-        pairs(body, lambda piece: mid_copy(block, unit, piece).start())
+        steps(body, lambda piece: mid_copy(block, unit, piece).start())
 
     def expand(block, unit):
         each(lambda piece: mid_copy(block, unit, piece).wait_recv())
@@ -271,7 +270,8 @@
 
         def body(piece):
             cols = columns(piece)
-            total = dot(mid[unit], w_two[block % 2, :, cols])
+            total = dot(mid[unit, :, :channels], w_two[block % 2, :channels, cols])
+            total += dot(mid[unit, :, channels:], w_two[block % 2, channels:, cols])
             total = gains[block, 2, cols] * total + biases[block, 2, cols]
             values = jnp.maximum(total + cur[unit, :, own_columns(piece)].astype(jnp.float32), 0.0)
             cur[unit, :, own_columns(piece)] = values.astype(jnp.bfloat16)
@@ -282,7 +282,7 @@
             else:
                 outward(unit, piece).start()
 
-        pairs(body, after)
+        steps(body, after)
         if block == blocks - 1:
             home(unit).start()
 

time: 116 us -> 113 us (0.974)
  Pallas kernels: 113 us -> 110 us
    pallas_call x1, Pallas kernels: 113 us -> 110 us  [call(): pl.pallas_call(functools.partial(fused_kernel, count), out_shape=jax.Shap...]
where the time goes in v4:
time: 113 us
  Pallas kernels  110 us (97%)
  local copies, waits for them, and re-layouts  3.14 us (3%)
    pallas_call x1, Pallas kernels, call(): pl.pallas_call(functools.partial(fused_kernel, count), out_shape=jax.Shap...  110 us
    unnamed x1, local copies, waits for them, and re-layouts  3.14 us

profile of v4, /device:TPU:13, one launch (start us, length us, event | category | flops | bytes accessed | tf_op | source)
XLA Modules:
  0.0 112.8 jit_solution(13946220779617850107)
XLA Ops:
  0.0 109.7 %shard_map.64 = bf16[4,256,1024]{2,1,0:T(8,128)(2,1)} custom-call(bf16[4,256,1024]{2,1,0:T(8,128)(2,1)} %bitcast.4, bf16[3,2048,1024]{2,1,0:T(8,128)(2,1)} %w_reduce.1, bf16[3,288,1024]{2,1,0:T(8,128)(2,1)} %bitcast.5, bf16[3,2048,1024]{2,1,0:T(8,128)(2,1)} %w_expand.1, f32[3,3,1024]{2,1,0:T(4,128)} %gains.1, f32[3,3,1024]{2,1,0:T(4,128)} %biases.1), custom_call_target="tpu_custom_call" | custom-call | flops 40265318400 | bytes 25165824 | tf_op jit(solution)/shard_map/pallas_call | solution.py:423
  109.7 3.1 %copy.8 = bf16[4,4,64,1024]{3,2,1,0:T(8,128)(2,1)} copy(bf16[4,4,64,1024]{3,2,1,0:T(8,128)(2,1)} %bitcast.3) | data formatting | bytes 4194304
